TPU v7x, 32 devices: a whole 2x2x4 slice. The times are simulated.
32 devices in a mesh: dp: 16 (over z, y, x), mp: 2 (over core).
Axes of the slice: x: 2, y: 2, z: 4, core: 2. Of those that a mesh axis runs over, the one named last changes fastest.
Arguments:
- patches: bfloat16 [12544, 768], P(('dp', 'mp')), may hold values from -6 to 6
- cotangent: bfloat16 [12544, 768], P(('dp', 'mp')), may hold values from -6 to 6
- patch_counts: int32 [64], P('dp'), may hold values from 0 to 576, as said below
- qkv_weight: float32 [2, 768, 3, 768], P(None, 'dp', None, 'mp'), may hold values from -0.21875 to 0.21875
- out_weight: float32 [2, 768, 768], P(None, 'mp', 'dp'), may hold values from -1.5 to 1.5
- up_weight: float32 [2, 768, 3072], P(None, 'dp', 'mp'), may hold values from -0.21875 to 0.21875
- down_weight: float32 [2, 3072, 768], P(None, 'mp', 'dp'), may hold values from -0.109375 to 0.109375
- norms: float32 [2, 4, 768], replicated
- qkv_rows: float32 [2, 768], P(None, 'dp'), may hold values from 1568 to 25088
- qkv_cols: float32 [2, 3, 768], P(None, None, 'mp'), may hold values from 1568 to 25088
- out_rows: float32 [2, 768], P(None, 'mp'), may hold values from 1568 to 50176
- out_cols: float32 [2, 768], P(None, 'dp'), may hold values from 1568 to 50176
- up_rows: float32 [2, 768], P(None, 'dp'), may hold values from 196 to 3136
- up_cols: float32 [2, 3072], P(None, 'mp'), may hold values from 196 to 3136
- down_rows: float32 [2, 3072], P(None, 'mp'), may hold values from 1045 to 12544
- down_cols: float32 [2, 768], P(None, 'dp'), may hold values from 1045 to 12544
- norm_state: float32 [2, 4, 768], P(None, None, 'dp'), may hold values from 1568 to 25088
Outputs:
- activations: bfloat16 [12544, 768], P(('dp', 'mp'))
- input_grad: float32 [12544, 768], P(('dp', 'mp'))
- qkv_grad: float32 [2, 768, 3, 768], P(None, 'dp', None, 'mp')
- out_grad: float32 [2, 768, 768], P(None, 'mp', 'dp')
- up_grad: float32 [2, 768, 3072], P(None, 'dp', 'mp')
- down_grad: float32 [2, 3072, 768], P(None, 'mp', 'dp')
- norm_grad: float32 [2, 4, 768], P(None, None, 'dp')
- qkv_new: float32 [2, 768, 3, 768], P(None, 'dp', None, 'mp')
- out_new: float32 [2, 768, 768], P(None, 'mp', 'dp')
- up_new: float32 [2, 768, 3072], P(None, 'dp', 'mp')
- down_new: float32 [2, 3072, 768], P(None, 'mp', 'dp')
- norm_new: float32 [2, 4, 768], P(None, None, 'dp')
- qkv_copy: bfloat16 [2, 768, 3, 768], P(None, 'dp', None, 'mp')
- out_copy: bfloat16 [2, 768, 768], P(None, 'mp', 'dp')
- up_copy: bfloat16 [2, 768, 3072], P(None, 'dp', 'mp')
- down_copy: bfloat16 [2, 3072, 768], P(None, 'mp', 'dp')
- qkv_rows_new: float32 [2, 768], P(None, 'dp')
- qkv_cols_new: float32 [2, 3, 768], P(None, None, 'mp')
- out_rows_new: float32 [2, 768], P(None, 'mp')
- out_cols_new: float32 [2, 768], P(None, 'dp')
- up_rows_new: float32 [2, 768], P(None, 'dp')
- up_cols_new: float32 [2, 3072], P(None, 'mp')
- down_rows_new: float32 [2, 3072], P(None, 'mp')
- down_cols_new: float32 [2, 768], P(None, 'dp')
- attention_moments: float32 [2, 2, 768], P(None, None, 'dp')
- feedforward_moments: float32 [2, 2, 768], P(None, None, 'dp')
- update_rms: float32 [2, 8], replicated
Inputs may be any that keep to these rules, and one draw needn't show every extreme that they name: `patch_counts`: each index of dp owns 4 slots in a row; they list its 384 px images (576 patches) first, then its 224 px images (196 patches), then empty slots (0). The patches of one index of dp total at most 784, exactly 784 on some index in every draw, and half of 784 or more on every index; some index holds a 384 px image in every draw.
All inputs are finite; a program needn't handle non-finite values.
Results may differ from a plain program's by a relative error of at most 0.028.
Values may be sent and summed in bfloat16 or wider, within the bound.
A program may use at most 256 MiB of HBM per device.

v0:
```python
import jax
import jax.numpy as jnp
from jax import lax
from jax.sharding import PartitionSpec as P

D = 768
HEAD_DIM = 64
FF = 3072


DECAY = 0.5
EPS_SQUARE = 1e-30
CLIP = 0.25
RATE = 2.0
MASKED = -1e30


def for_sending(value):
    return jax.tree.map(lambda a: a.astype(jnp.bfloat16) if a.dtype == jnp.float32 else a, value)


def layer_norm(rows, gain, shift):
    centre = rows - jnp.mean(rows, axis=-1, keepdims=True)
    spread = jnp.mean(centre * centre, axis=-1, keepdims=True)
    return centre * lax.rsqrt(spread + 1e-06) * gain + shift


def norm_back(rows, gain, shift, grad):
    result, back = jax.vjp(layer_norm, rows, gain, shift)
    return back(grad)


def exact_gelu(values):
    return jax.nn.gelu(values, approximate=False)


def segments(counts, length):
    bounds = jnp.cumsum(counts)
    places = jnp.arange(length, dtype=jnp.int32)
    image = jnp.sum((places[:, None] >= bounds[None, :]).astype(jnp.int32), axis=1)
    live = (places < bounds[-1]).astype(jnp.float32)
    return (image[:, None] == image[None, :], live)


def attention_scores(query, keys, same):
    scale = query.shape[-1] ** (-0.5)
    scores = jnp.einsum("qhd,khd->hqk", query, keys, preferred_element_type=jnp.float32) * scale
    return jnp.where(same[None], scores, MASKED)


def attend(qkv, same):
    scores = attention_scores(qkv[:, 0], qkv[:, 1], same)
    top = jnp.max(scores, axis=-1, keepdims=True)
    raised = jnp.exp(scores - top)
    total = jnp.sum(raised, axis=-1, keepdims=True)
    probs = (raised / total).astype(jnp.bfloat16)
    mixed = jnp.einsum("hqk,khd->qhd", probs, qkv[:, 2], preferred_element_type=jnp.float32)
    return (mixed.reshape(mixed.shape[0], -1), top + jnp.log(total))


def attend_back(qkv, same, log_total, grad_mixed):
    query, keys, values = (qkv[:, 0], qkv[:, 1], qkv[:, 2])
    scale = query.shape[-1] ** (-0.5)
    probs = jnp.exp(attention_scores(query, keys, same) - log_total)
    d_values = jnp.einsum(
        "hqk,qhd->khd", probs.astype(jnp.bfloat16), grad_mixed, preferred_element_type=jnp.float32
    )
    d_probs = jnp.einsum("qhd,khd->hqk", grad_mixed, values, preferred_element_type=jnp.float32)
    d_scores = (probs * (d_probs - jnp.sum(probs * d_probs, axis=-1, keepdims=True))).astype(
        jnp.bfloat16
    )
    d_query = jnp.einsum("hqk,khd->qhd", d_scores, keys, preferred_element_type=jnp.float32) * scale
    d_keys = jnp.einsum("hqk,qhd->khd", d_scores, query, preferred_element_type=jnp.float32) * scale
    return jnp.stack([d_query, d_keys, d_values], axis=1).astype(jnp.bfloat16)


def spread_rows(values):
    return lax.all_gather(values, "mp", axis=0, tiled=True)


def size_of(name):
    return lax.axis_size("dp") if name == "dp" else lax.axis_size("mp")


def per_device(
    patches,
    cotangent,
    patch_counts,
    qkv_weight,
    out_weight,
    up_weight,
    down_weight,
    norms,
    qkv_rows,
    qkv_cols,
    out_rows,
    out_cols,
    up_rows,
    up_cols,
    down_rows,
    down_cols,
    norm_state,
):
    layers = qkv_weight.shape[0]
    half = patches.shape[0]
    length = half * lax.axis_size("mp")
    same, live_all = segments(patch_counts, length)
    live = lax.dynamic_slice_in_dim(live_all, lax.axis_index("mp") * half, half)
    rows = patches.astype(jnp.float32)
    kept = []
    for layer in range(layers):
        pieces = (
            qkv_weight[layer].astype(jnp.bfloat16),
            out_weight[layer].astype(jnp.bfloat16),
            up_weight[layer].astype(jnp.bfloat16),
            down_weight[layer].astype(jnp.bfloat16),
        )
        whole = (
            lax.all_gather(pieces[0], "dp", axis=0, tiled=True),
            lax.all_gather(pieces[1], "dp", axis=1, tiled=True),
            lax.all_gather(pieces[2], "dp", axis=0, tiled=True),
            lax.all_gather(pieces[3], "dp", axis=1, tiled=True),
        )
        w_qkv, w_out, w_up, w_down = whole
        local = w_qkv.shape[2]
        normed_a = spread_rows(
            layer_norm(rows, norms[layer, 0], norms[layer, 1]).astype(jnp.bfloat16)
        )
        qkv = jnp.dot(normed_a, w_qkv.reshape(D, 3 * local), preferred_element_type=jnp.float32)
        qkv = qkv.astype(jnp.bfloat16).reshape(length, 3, local // HEAD_DIM, HEAD_DIM)
        mixed, log_total = attend(qkv, same)
        mixed = mixed.astype(jnp.bfloat16)
        middle = rows + lax.psum_scatter(
            jnp.dot(mixed, w_out, preferred_element_type=jnp.float32).astype(jnp.bfloat16),
            "mp",
            scatter_dimension=0,
            tiled=True,
        ).astype(jnp.float32)
        normed_b = spread_rows(
            layer_norm(middle, norms[layer, 2], norms[layer, 3]).astype(jnp.bfloat16)
        )
        hidden = jnp.dot(normed_b, w_up, preferred_element_type=jnp.float32)
        active = exact_gelu(hidden).astype(jnp.bfloat16)
        after = middle + lax.psum_scatter(
            jnp.dot(active, w_down, preferred_element_type=jnp.float32).astype(jnp.bfloat16),
            "mp",
            scatter_dimension=0,
            tiled=True,
        ).astype(jnp.float32)
        stored = None
        kept.append(
            (
                rows,
                normed_a,
                qkv,
                log_total,
                mixed,
                middle,
                normed_b,
                hidden,
                active,
                stored,
                pieces,
            )
        )
        rows = after
    activations = rows.astype(jnp.bfloat16)
    grad = cotangent.astype(jnp.float32) * live[:, None]
    reduced = [None] * layers
    for layer in reversed(range(layers)):
        (
            rows_in,
            normed_a,
            qkv,
            log_total,
            mixed,
            middle,
            normed_b,
            hidden,
            active,
            stored,
            pieces,
        ) = kept[layer]
        whole = (
            lax.all_gather(pieces[0], "dp", axis=0, tiled=True),
            lax.all_gather(pieces[1], "dp", axis=1, tiled=True),
            lax.all_gather(pieces[2], "dp", axis=0, tiled=True),
            lax.all_gather(pieces[3], "dp", axis=1, tiled=True),
        )
        w_qkv, w_out, w_up, w_down = whole
        local = w_qkv.shape[2]
        grad_down = spread_rows(grad.astype(jnp.bfloat16))
        g_down = jnp.einsum("tf,td->fd", active, grad_down, preferred_element_type=jnp.float32)
        d_active = jnp.einsum("td,fd->tf", grad_down, w_down, preferred_element_type=jnp.float32)
        gelu_value, gelu_back = jax.vjp(exact_gelu, hidden)
        d_hidden = gelu_back(d_active)[0].astype(jnp.bfloat16)
        g_up = jnp.einsum("td,tf->df", normed_b, d_hidden, preferred_element_type=jnp.float32)
        d_normed_b = lax.psum_scatter(
            jnp.einsum("tf,df->td", d_hidden, w_up, preferred_element_type=jnp.float32).astype(
                jnp.bfloat16
            ),
            "mp",
            scatter_dimension=0,
            tiled=True,
        ).astype(jnp.float32)
        d_middle, g_gain_b, g_shift_b = norm_back(
            middle, norms[layer, 2], norms[layer, 3], d_normed_b
        )
        grad_mid = grad + d_middle
        grad_out = spread_rows(grad_mid.astype(jnp.bfloat16))
        g_out = jnp.einsum("tc,td->cd", mixed, grad_out, preferred_element_type=jnp.float32)
        d_mixed = jnp.einsum(
            "td,cd->tc", grad_out, w_out, preferred_element_type=jnp.float32
        ).astype(jnp.bfloat16)
        d_qkv = attend_back(
            qkv, same, log_total, d_mixed.reshape(length, local // HEAD_DIM, HEAD_DIM)
        )
        d_qkv = d_qkv.reshape(length, 3 * local)
        g_qkv = jnp.einsum(
            "td,tc->dc", normed_a, d_qkv, preferred_element_type=jnp.float32
        ).reshape(D, 3, local)
        d_normed_a = lax.psum_scatter(
            jnp.einsum(
                "tc,dc->td", d_qkv, w_qkv.reshape(D, 3 * local), preferred_element_type=jnp.float32
            ).astype(jnp.bfloat16),
            "mp",
            scatter_dimension=0,
            tiled=True,
        ).astype(jnp.float32)
        d_input, g_gain_a, g_shift_a = norm_back(
            rows_in, norms[layer, 0], norms[layer, 1], d_normed_a
        )
        grad = grad_mid + d_input
        norm_terms = jnp.stack([g_gain_a, g_shift_a, g_gain_b, g_shift_b])
        reduced[layer] = (
            lax.psum_scatter(g_qkv, "dp", scatter_dimension=0, tiled=True),
            lax.psum_scatter(g_out, "dp", scatter_dimension=1, tiled=True),
            lax.psum_scatter(g_up, "dp", scatter_dimension=0, tiled=True),
            lax.psum_scatter(g_down, "dp", scatter_dimension=1, tiled=True),
            lax.psum_scatter(norm_terms, "dp", scatter_dimension=1, tiled=True),
        )
    col_axes = ("mp", "dp", "mp", "dp")
    row_counts = (D, D, D, FF)
    col_counts = (3 * D, D, FF, D)
    masters = (qkv_weight, out_weight, up_weight, down_weight)
    row_states = (qkv_rows, out_rows, up_rows, down_rows)
    col_states = (qkv_cols, out_cols, up_cols, down_cols)
    entries = [(layer, which) for layer in range(layers) for which in range(4)]
    grads = [reduced[layer][which] for layer, which in entries]
    row_olds = [row_states[which][layer] for layer, which in entries]
    col_olds = [col_states[which][layer] for layer, which in entries]
    norm_partial = jnp.stack([reduced[layer][4] for layer in range(layers)])
    width = norm_state.shape[2]
    row_parts, col_parts = ([], [])
    for position, (layer, which) in enumerate(entries):
        matrix = grads[position].reshape(grads[position].shape[0], -1)
        square = matrix * matrix + EPS_SQUARE
        row_parts.append(jnp.sum(square, axis=1))
        col_parts.append(jnp.sum(square, axis=0).reshape(col_olds[position].shape))
    model_side = tuple(
        [
            row_parts[position] if col_axes[which] == "mp" else col_parts[position]
            for position, (layer, which) in enumerate(entries)
        ]
        + [norm_partial]
    )
    data_side = tuple(
        (
            col_parts[position] if col_axes[which] == "mp" else row_parts[position]
            for position, (layer, which) in enumerate(entries)
        )
    )
    model_sums = jax.tree.map(
        lambda part: part.astype(jnp.float32), lax.psum(for_sending(model_side), "mp")
    )
    data_sums = lax.psum(data_side, "dp")
    norm_grad = model_sums[len(entries)]
    row_sums = [
        model_sums[position] if col_axes[which] == "mp" else data_sums[position]
        for position, (layer, which) in enumerate(entries)
    ]
    col_sums = [
        data_sums[position] if col_axes[which] == "mp" else model_sums[position]
        for position, (layer, which) in enumerate(entries)
    ]
    row_news = [
        DECAY * row_olds[position] + (1.0 - DECAY) * row_sums[position] / col_counts[which]
        for position, (layer, which) in enumerate(entries)
    ]
    shares = jnp.stack(
        [
            jnp.sum(row_news[position]) / size_of(col_axes[which])
            for position, (layer, which) in enumerate(entries)
        ]
    )
    row_totals = lax.psum(shares, ("dp", "mp"))
    row_means = [
        row_totals[position] / row_counts[which] for position, (layer, which) in enumerate(entries)
    ]
    col_news = [
        DECAY * col_olds[position] + (1.0 - DECAY) * col_sums[position] / row_counts[which]
        for position, (layer, which) in enumerate(entries)
    ]
    directions, step_parts, weight_parts = ([], [], [])
    for position, (layer, which) in enumerate(entries):
        matrix = grads[position].reshape(grads[position].shape[0], -1)
        second = (
            row_news[position][:, None] * col_news[position].reshape(1, -1) / row_means[position]
        )
        direction = matrix * lax.rsqrt(second)
        directions.append(direction)
        step_parts.append(jnp.sum(direction * direction))
        master = masters[which][layer]
        weight_parts.append(jnp.sum(master * master))
    own_norms = lax.dynamic_slice_in_dim(norms, lax.axis_index("dp") * width, width, 2)
    norm_state_new = DECAY * norm_state + (1.0 - DECAY) * (norm_grad * norm_grad + EPS_SQUARE)
    norm_dirs = norm_grad * lax.rsqrt(norm_state_new)
    norm_parts = jnp.sum(norm_dirs * norm_dirs, axis=2) / lax.axis_size("mp")
    step_all = jnp.concatenate(
        [jnp.stack(step_parts).reshape(layers, 4), norm_parts], axis=1
    ).reshape(-1)
    step_total, weight_total = lax.psum((step_all, jnp.stack(weight_parts)), ("dp", "mp"))
    step_total = step_total.reshape(layers, 8)
    matrix_counts = jnp.asarray(
        [float(row_counts[which] * col_counts[which]) for which in range(4)], jnp.float32
    )
    update_rms = jnp.concatenate(
        [jnp.sqrt(step_total[:, :4] / matrix_counts[None, :]), jnp.sqrt(step_total[:, 4:] / D)],
        axis=1,
    )
    news = [[None] * layers for which in range(4)]
    rows_new = [[None] * layers for which in range(4)]
    cols_new = [[None] * layers for which in range(4)]
    for position, (layer, which) in enumerate(entries):
        master = masters[which][layer]
        scale = jnp.sqrt(weight_total[position] / (row_counts[which] * col_counts[which]) + 1e-06)
        clipped = directions[position] / jnp.maximum(1.0, update_rms[layer, which] / CLIP)
        news[which][layer] = master - RATE * scale * clipped.reshape(master.shape)
        rows_new[which][layer] = row_news[position]
        cols_new[which][layer] = col_news[position]
    norm_scale = jnp.sqrt(jnp.mean(norms * norms, axis=2) + 1e-06)
    norm_clipped = norm_dirs / jnp.maximum(1.0, update_rms[:, 4:] / CLIP)[:, :, None]
    norm_new = own_norms - RATE * norm_scale[:, :, None] * norm_clipped
    grad_out = [jnp.stack([reduced[layer][which] for layer in range(layers)]) for which in range(4)]
    new_out = [jnp.stack(news[which]) for which in range(4)]
    row_out = [jnp.stack(rows_new[which]) for which in range(4)]
    col_out = [jnp.stack(cols_new[which]) for which in range(4)]
    return (
        activations,
        grad,
        grad_out[0],
        grad_out[1],
        grad_out[2],
        grad_out[3],
        norm_grad,
        new_out[0],
        new_out[1],
        new_out[2],
        new_out[3],
        norm_new,
        new_out[0].astype(jnp.bfloat16),
        new_out[1].astype(jnp.bfloat16),
        new_out[2].astype(jnp.bfloat16),
        new_out[3].astype(jnp.bfloat16),
        row_out[0],
        col_out[0],
        row_out[1],
        col_out[1],
        row_out[2],
        col_out[2],
        row_out[3],
        col_out[3],
        norm_state_new[:, 0:2],
        norm_state_new[:, 2:4],
        update_rms,
    )


def solution(mesh):
    in_specs = (
        P(("dp", "mp"), None),
        P(("dp", "mp"), None),
        P("dp"),
        P(None, "dp", None, "mp"),
        P(None, "mp", "dp"),
        P(None, "dp", "mp"),
        P(None, "mp", "dp"),
        P(),
        P(None, "dp"),
        P(None, None, "mp"),
        P(None, "mp"),
        P(None, "dp"),
        P(None, "dp"),
        P(None, "mp"),
        P(None, "mp"),
        P(None, "dp"),
        P(None, None, "dp"),
    )
    out_specs = (
        P(("dp", "mp"), None),
        P(("dp", "mp"), None),
        P(None, "dp", None, "mp"),
        P(None, "mp", "dp"),
        P(None, "dp", "mp"),
        P(None, "mp", "dp"),
        P(None, None, "dp"),
        P(None, "dp", None, "mp"),
        P(None, "mp", "dp"),
        P(None, "dp", "mp"),
        P(None, "mp", "dp"),
        P(None, None, "dp"),
        P(None, "dp", None, "mp"),
        P(None, "mp", "dp"),
        P(None, "dp", "mp"),
        P(None, "mp", "dp"),
        P(None, "dp"),
        P(None, None, "mp"),
        P(None, "mp"),
        P(None, "dp"),
        P(None, "dp"),
        P(None, "mp"),
        P(None, "mp"),
        P(None, "dp"),
        P(None, None, "dp"),
        P(None, None, "dp"),
        P(),
    )
    return jax.shard_map(
        per_device, mesh=mesh, in_specs=in_specs, out_specs=out_specs, check_vma=False
    )
```

profile of v0, /device:TPU:0, one launch (start us, length us, event | category | flops | bytes accessed | tf_op | source)
XLA Modules:
  0.0 2358.5 jit_solution(13068306011847010134)
XLA Ops:
  14.8 50.2 %all_gather.58 = bf16[384,768]{0,1:T(8,128)(2,1)} all-gather(bf16[384,48]{0,1:T(8,128)(2,1)S(1)} %get-tuple-element.231), channel_id=1, replica_groups=mesh['dp'=16,'mp'=2] {'dp'}, dimensions={1}, use_global_device_ids=true | all-gather | bytes 626688 | tf_op jit(solution)/shard_map/all_gather | solution.py:120
  133.9 61.8 %all-gather.21.cloned.1.call-done = bf16[768,1536]{1,0:T(8,128)(2,1)} async-done(((bf16[48,1536]{1,0:T(8,128)(2,1)}), bf16[768,1536]{1,0:T(8,128)(2,1)}) %all-gather.21.cloned.1.call-update) | async-done | bytes 2359312 | tf_op jit(solution)/shard_map/all_gather | solution.py:121
  195.6 10.1 all-gather.19.cloned.1.call-done
  205.7 15.5 multiply_convert_fusion.3
  221.2 51.2 %all-gather.23.cloned.1.call-done = bf16[1536,768]{0,1:T(8,128)(2,1)} async-done(((bf16[1536,48]{0,1:T(8,128)(2,1)}), bf16[1536,768]{0,1:T(8,128)(2,1)}) %all-gather.23.cloned.1.call-update) | async-done | bytes 2359312 | tf_op jit(solution)/shard_map/all_gather | solution.py:122
  288.5 46.2 %all_gather.64 = bf16[384,768]{0,1:T(8,128)(2,1)S(1)} all-gather(bf16[384,48]{0,1:T(8,128)(2,1)S(1)} %get-tuple-element.230), channel_id=1, replica_groups=mesh['dp'=16,'mp'=2] {'dp'}, dimensions={1}, use_global_device_ids=true | all-gather | bytes 626688 | tf_op jit(solution)/shard_map/all_gather | solution.py:120
  334.7 15.7 all-gather.27.cloned.1.call-done
  369.5 10.0 fusion.138
  415.3 61.0 %all-gather.31.cloned.1.call-done = bf16[768,1536]{1,0:T(8,128)(2,1)} async-done(((bf16[48,1536]{1,0:T(8,128)(2,1)}), bf16[768,1536]{1,0:T(8,128)(2,1)}) %all-gather.31.cloned.1.call-update) | async-done | bytes 2359312 | tf_op jit(solution)/shard_map/all_gather | solution.py:121
  476.3 10.1 all-gather.29.cloned.1.call-done
  499.0 66.7 %all-gather.33.cloned.1.call-done = bf16[1536,768]{0,1:T(8,128)(2,1)} async-done(((bf16[1536,48]{0,1:T(8,128)(2,1)}), bf16[1536,768]{0,1:T(8,128)(2,1)}) %all-gather.33.cloned.1.call-update) | async-done | bytes 2359312 | tf_op jit(solution)/shard_map/all_gather | solution.py:122
  565.7 16.3 add_convert_fusion.1
  611.1 10.3 all-gather.37.cloned.1.call-done
  623.9 9.6 fusion.28
  633.5 13.3 multiply_reduce_fusion.1
  681.3 10.6 all-gather.39.cloned.1.call-done
  704.5 10.0 reduce-scatter.35.cloned.1.call-done
  718.5 10.5 all-gather.41.cloned.1.call-done
  742.0 15.3 multiply_reduce_fusion
  844.2 72.8 %reduce-scatter.45.cloned.1.call-done = f32[384,48]{0,1:T(8,128)} async-done(((f32[384,768]{0,1:T(8,128)}), f32[384,48]{0,1:T(8,128)}) %reduce-scatter.45.cloned.1.call-update) | async-done | bytes 73744 | tf_op jit(solution)/shard_map/reduce_scatter | solution.py:237
  918.6 123.9 %reduce-scatter.57.cloned.1.call-done = f32[48,4]{1,0:T(8,128)} async-done(((f32[768,4]{1,0:T(8,128)}), f32[48,4]{1,0:T(8,128)}) %reduce-scatter.57.cloned.1.call-update) | async-done | bytes 784
  1043.4 142.0 %reduce-scatter.53.cloned.1.call-done = f32[1536,48]{0,1:T(8,128)} async-done(((f32[1536,768]{0,1:T(8,128)}), f32[1536,48]{0,1:T(8,128)}) %reduce-scatter.53.cloned.1.call-update) | async-done | bytes 294928 | tf_op jit(solution)/shard_map/reduce_scatter | solution.py:239
  1187.1 140.0 %reduce-scatter.49.cloned.1.call-done = f32[48,1536]{1,0:T(8,128)} async-done(((f32[768,1536]{1,0:T(8,128)}), f32[48,1536]{1,0:T(8,128)}) %reduce-scatter.49.cloned.1.call-update) | async-done | bytes 294928 | tf_op jit(solution)/shard_map/reduce_scatter | solution.py:238
  1328.7 137.5 %reduce-scatter.41.cloned.1.call-done = f32[48,3,384]{2,0,1:T(8,128)} async-done(((f32[768,3,384]{2,0,1:T(8,128)}), f32[48,3,384]{2,0,1:T(8,128)}) %reduce-scatter.41.cloned.1.call-update) | async-done | bytes 221200 | tf_op jit(solution)/shard_map/reduce_scatter | solution.py:236
  1467.8 127.5 %reduce-scatter.43.cloned.1.call-done = f32[384,48]{0,1:T(8,128)} async-done(((f32[384,768]{0,1:T(8,128)}), f32[384,48]{0,1:T(8,128)}) %reduce-scatter.43.cloned.1.call-update) | async-done | bytes 73744 | tf_op jit(solution)/shard_map/reduce_scatter | solution.py:237
  1601.7 120.0 %reduce-scatter.55.cloned.1.call-done = f32[48,4]{1,0:T(8,128)} async-done(((f32[768,4]{1,0:T(8,128)}), f32[48,4]{1,0:T(8,128)}) %reduce-scatter.55.cloned.1.call-update) | async-done | bytes 784
  1722.5 140.8 %reduce-scatter.47.cloned.1.call-done = f32[48,1536]{1,0:T(8,128)} async-done(((f32[768,1536]{1,0:T(8,128)}), f32[48,1536]{1,0:T(8,128)}) %reduce-scatter.47.cloned.1.call-update) | async-done | bytes 294928 | tf_op jit(solution)/shard_map/reduce_scatter | solution.py:238
  1864.4 142.0 %reduce-scatter.51.cloned.1.call-done = f32[1536,48]{0,1:T(8,128)} async-done(((f32[1536,768]{0,1:T(8,128)}), f32[1536,48]{0,1:T(8,128)}) %reduce-scatter.51.cloned.1.call-update) | async-done | bytes 294928 | tf_op jit(solution)/shard_map/reduce_scatter | solution.py:239
  2011.5 133.5 %reduce-scatter.39.cloned.1.call-done = f32[48,3,384]{2,0,1:T(8,128)} async-done(((f32[768,3,384]{2,0,1:T(8,128)}), f32[48,3,384]{2,0,1:T(8,128)}) %reduce-scatter.39.cloned.1.call-update) | async-done | bytes 221200 | tf_op jit(solution)/shard_map/reduce_scatter | solution.py:236
  2146.1 75.6 %all-reduce.1 = (f32[384]{0:T(512)S(1)}, f32[1536]{0:T(1024)S(1)}, f32[384]{0:T(512)S(1)}, f32[1536]{0:T(1024)S(1)}, f32[3,384]{1,0:T(4,128)S(1)}, /*index=5*/f3...) all-reduce(f32[384]{0:T(512)S(1)} %copy-done.97, ...), channel_id=1, replica_groups=mesh['dp'=16,'mp'=2] {'dp'}, use_global_device_ids=true, to_apply=%region_66.67 | all-reduce | flops 9216 | bytes 73728 | tf_op jit(solution)/shard_map/psum | solution.py:276
  2231.4 36.9 %psum.151 = f32[8]{0:T(128)S(1)} all-reduce(f32[8]{0:T(128)S(1)} %stack.305), channel_id=1, replica_groups=mesh['dp'=16,'mp'=2] {'dp','mp'}, use_global_device_ids=true, to_apply=%region_86.87 | all-reduce | flops 8 | bytes 64 | tf_op jit(solution)/shard_map/psum | solution.py:296
  2287.3 41.1 %all-reduce = (f32[2,8]{1,0:T(2,128)S(1)}, f32[8]{0:T(128)S(1)}) all-reduce(f32[2,8]{1,0:T(2,128)S(1)} %pad_maximum_fusion.15, f32[8]{0:T(128)S(1)} %copy-done.111), channel_id=1, replica_groups=mesh['dp'=16,'mp'=2] {'dp','mp'}, use_global_device_ids=true, to_apply=%region_110.111 | all-reduce | flops 24 | bytes 192 | tf_op jit(solution)/shard_map/psum | solution.py:322
  (522 shorter events, 393.2 us)
Async XLA Ops:
  7.2 66.9 %all-gather.17.cloned.1.call-start = ((), (), s32[]{:S(2)}) async-start(), calls=%async_computation.19 | async-start | bytes 1880064 | tf_op jit(solution)/shard_map/all_gather | solution.py:119
  9.1 75.2 %all-gather.15.cloned.1.call-start = ((), (), s32[]{:S(2)}) async-start(), calls=%async_computation.18 | async-start | bytes 1806336 | tf_op jit(solution)/shard_map/all_gather | solution.py:78
  14.0 114.9 %reduce-scatter.23.cloned.1.call-start = ((), (), s32[]{:S(2)}) async-start(), calls=%async_computation.20 | async-start | bytes 1806336 | tf_op jit(solution)/shard_map/reduce_scatter | solution.py:133
  118.9 76.8 %all-gather.21.cloned.1.call-start = ((), (), s32[]{:S(2)}) async-start(), calls=%async_computation.22 | async-start | bytes 2506752 | tf_op jit(solution)/shard_map/all_gather | solution.py:121
  119.7 86.0 %all-gather.19.cloned.1.call-start = ((), (), s32[]{:S(2)}) async-start(), calls=%async_computation.21 | async-start | bytes 1806336 | tf_op jit(solution)/shard_map/all_gather | solution.py:78
  133.0 139.4 %all-gather.23.cloned.1.call-start = ((), (), s32[]{:S(2)}) async-start(), calls=%async_computation.23 | async-start | bytes 2506752 | tf_op jit(solution)/shard_map/all_gather | solution.py:122
  133.8 151.8 %reduce-scatter.25.cloned.1.call-start = ((), (), s32[]{:S(2)}) async-start(), calls=%async_computation.24 | async-start | bytes 1806336 | tf_op jit(solution)/shard_map/reduce_scatter | solution.py:144
  277.9 72.5 %all-gather.27.cloned.1.call-start = ((), (), s32[]{:S(2)}) async-start(), calls=%async_computation.26 | async-start | bytes 1880064 | tf_op jit(solution)/shard_map/all_gather | solution.py:119
  278.7 81.9 %all-gather.25.cloned.1.call-start = ((), (), s32[]{:S(2)}) async-start(), calls=%async_computation.25 | async-start | bytes 1806336 | tf_op jit(solution)/shard_map/all_gather | solution.py:78
  288.4 121.0 %reduce-scatter.27.cloned.1.call-start = ((), (), s32[]{:S(2)}) async-start(), calls=%async_computation.27 | async-start | bytes 1806336 | tf_op jit(solution)/shard_map/reduce_scatter | solution.py:133
  399.4 76.9 %all-gather.31.cloned.1.call-start = ((), (), s32[]{:S(2)}) async-start(), calls=%async_computation.29 | async-start | bytes 2506752 | tf_op jit(solution)/shard_map/all_gather | solution.py:121
  400.1 86.3 %all-gather.29.cloned.1.call-start = ((), (), s32[]{:S(2)}) async-start(), calls=%async_computation.28 | async-start | bytes 1806336 | tf_op jit(solution)/shard_map/all_gather | solution.py:78
  412.1 86.9 %all-gather.35.cloned.1.call-start = ((), (), s32[]{:S(2)}) async-start(), calls=%async_computation.32 | async-start | bytes 1806336 | tf_op jit(solution)/shard_map/all_gather | solution.py:78
  414.5 151.2 %all-gather.33.cloned.1.call-start = ((), (), s32[]{:S(2)}) async-start(), calls=%async_computation.30 | async-start | bytes 2506752 | tf_op jit(solution)/shard_map/all_gather | solution.py:122
  415.1 181.3 %reduce-scatter.31.cloned.1.call-start = ((), (), s32[]{:S(2)}) async-start(), calls=%async_computation.33 | async-start | bytes 1806336 | tf_op jit(solution)/shard_map/reduce_scatter | solution.py:198
  586.5 19.7 reduce-scatter.29.cloned.1.call-start
  596.3 25.1 %all-gather.37.cloned.1.call-start = ((), (), s32[]{:S(2)}) async-start(), calls=%async_computation.34 | async-start | bytes 1806336 | tf_op jit(solution)/shard_map/all_gather | solution.py:78
  610.8 65.5 %reduce-scatter.33.cloned.1.call-start = ((), (), s32[]{:S(2)}) async-start(), calls=%async_computation.35 | async-start | bytes 1806336 | tf_op jit(solution)/shard_map/reduce_scatter | solution.py:222
  666.3 25.6 %all-gather.39.cloned.1.call-start = ((), (), s32[]{:S(2)}) async-start(), calls=%async_computation.36 | async-start | bytes 1806336 | tf_op jit(solution)/shard_map/all_gather | solution.py:78
  681.3 33.2 %reduce-scatter.35.cloned.1.call-start = ((), (), s32[]{:S(2)}) async-start(), calls=%async_computation.37 | async-start | bytes 1806336 | tf_op jit(solution)/shard_map/reduce_scatter | solution.py:198
  704.5 24.5 %all-gather.41.cloned.1.call-start = ((), (), s32[]{:S(2)}) async-start(), calls=%async_computation.38 | async-start | bytes 1806336 | tf_op jit(solution)/shard_map/all_gather | solution.py:78
  718.4 86.9 %reduce-scatter.37.cloned.1.call-start = ((), (), s32[]{:S(2)}) async-start(), calls=%async_computation.39 | async-start | bytes 1806336 | tf_op jit(solution)/shard_map/reduce_scatter | solution.py:222
  776.7 140.3 %reduce-scatter.45.cloned.1.call-start = ((), (), s32[]{:S(2)}) async-start(), calls=%async_computation.43 | async-start | bytes 1253376 | tf_op jit(solution)/shard_map/reduce_scatter | solution.py:237
  780.5 262.0 %reduce-scatter.57.cloned.1.call-start = ((), (), s32[]{:S(2)}) async-start(), calls=%async_computation.49 | async-start | bytes 417792
  781.6 403.7 %reduce-scatter.53.cloned.1.call-start = ((), (), s32[]{:S(2)}) async-start(), calls=%async_computation.47 | async-start | bytes 5013504 | tf_op jit(solution)/shard_map/reduce_scatter | solution.py:239
  787.4 539.7 %reduce-scatter.49.cloned.1.call-start = ((), (), s32[]{:S(2)}) async-start(), calls=%async_computation.45 | async-start | bytes 5013504 | tf_op jit(solution)/shard_map/reduce_scatter | solution.py:238
  794.8 671.4 %reduce-scatter.41.cloned.1.call-start = ((), (), s32[]{:S(2)}) async-start(), calls=%async_computation.41 | async-start | bytes 3760128 | tf_op jit(solution)/shard_map/reduce_scatter | solution.py:236
  801.7 793.6 %reduce-scatter.43.cloned.1.call-start = ((), (), s32[]{:S(2)}) async-start(), calls=%async_computation.42 | async-start | bytes 1253376 | tf_op jit(solution)/shard_map/reduce_scatter | solution.py:237
  805.2 916.5 %reduce-scatter.55.cloned.1.call-start = ((), (), s32[]{:S(2)}) async-start(), calls=%async_computation.48 | async-start | bytes 417792
  809.8 1053.5 %reduce-scatter.47.cloned.1.call-start = ((), (), s32[]{:S(2)}) async-start(), calls=%async_computation.44 | async-start | bytes 5013504 | tf_op jit(solution)/shard_map/reduce_scatter | solution.py:238
  815.5 1190.9 %reduce-scatter.51.cloned.1.call-start = ((), (), s32[]{:S(2)}) async-start(), calls=%async_computation.46 | async-start | bytes 5013504 | tf_op jit(solution)/shard_map/reduce_scatter | solution.py:239
  822.8 1322.1 %reduce-scatter.39.cloned.1.call-start = ((), (), s32[]{:S(2)}) async-start(), calls=%async_computation.40 | async-start | bytes 3760128 | tf_op jit(solution)/shard_map/reduce_scatter | solution.py:236
  (129 other events, 20296.1 us)
Sparse Core Ops, SparseCore 0:
  11.3 62.7 all-gather.16
  76.3 8.0 all-gather.14
  119.0 9.8 reduce-scatter.22
  132.1 63.4 all-gather.20
  197.6 8.0 all-gather.18
  208.9 63.4 all-gather.22
  278.0 7.5 reduce-scatter.24
  288.8 61.4 all-gather.26
  352.5 8.0 all-gather.24
  399.5 9.8 reduce-scatter.26
  412.8 63.4 all-gather.30
  478.3 8.0 all-gather.28
  488.5 10.4 all-gather.34
  502.2 63.4 all-gather.32
  586.7 7.5 reduce-scatter.30
  596.4 9.7 reduce-scatter.28
  610.9 10.4 all-gather.36
  666.4 9.8 reduce-scatter.32
  681.4 10.4 all-gather.38
  704.6 9.8 reduce-scatter.34
  718.5 10.4 all-gather.40
  776.8 9.8 reduce-scatter.36
  791.5 125.4 reduce-scatter.44
  922.1 120.3 reduce-scatter.56
  1048.5 136.7 reduce-scatter.52
  1190.4 136.6 reduce-scatter.48
  1332.8 133.3 reduce-scatter.40
  1471.7 123.6 reduce-scatter.42
  1601.2 120.3 reduce-scatter.54
  1726.7 136.5 reduce-scatter.46
  1869.3 137.0 reduce-scatter.50
  2011.5 133.3 reduce-scatter.38
where the time goes:
time: 2370 us; the launch traced here: 2360 us
  waiting for transfers between devices  1670 us (70%)
  blocking collectives  252 us (11%)
  matrix products  220 us (9%)
  other arithmetic  117 us (5%)
  local copies, waits for them, and re-layouts  57.1 us (2%)
  between operations  37.4 us (2%)
    reduce_scatter x2, waiting for transfers between devices, per_device(): lax.psum_scatter(g_down, 'dp', scatter_dimension=1, tiled=True)  284 us
    reduce_scatter x2, waiting for transfers between devices, per_device(): lax.psum_scatter(g_up, 'dp', scatter_dimension=0, tiled=True)  281 us
    reduce_scatter x2, waiting for transfers between devices, per_device(): lax.psum_scatter(g_qkv, 'dp', scatter_dimension=0, tiled=True)  271 us
    unnamed x34, waiting for transfers between devices  246 us
    reduce_scatter x2, waiting for transfers between devices, per_device(): lax.psum_scatter(g_out, 'dp', scatter_dimension=1, tiled=True)  200 us
    all_gather x2, waiting for transfers between devices, per_device(): lax.all_gather(pieces[2], 'dp', axis=0, tiled=True)  123 us
    all_gather x2, waiting for transfers between devices, per_device(): lax.all_gather(pieces[3], 'dp', axis=1, tiled=True)  118 us
    all_gather x2, blocking collectives, per_device(): lax.all_gather(pieces[1], 'dp', axis=1, tiled=True)  96.4 us
  transfers between devices with their start and end apart: 32, of which 30 were waited for; matrix products, arithmetic and copies ran while one was open for 6% of the time, Pallas kernels for 0%

commit v1 on v0

--- a/solution.py
+++ b/solution.py
@@ -1,6 +1,10 @@
+import functools
+
 import jax
 import jax.numpy as jnp
 from jax import lax
+from jax.experimental import pallas as pl
+from jax.experimental.pallas import tpu as pltpu
 from jax.sharding import PartitionSpec as P
 
 D = 768
@@ -82,7 +86,627 @@
     return lax.axis_size("dp") if name == "dp" else lax.axis_size("mp")
 
 
-def per_device(
+TILE = 112
+VMEM_BYTES = 64 << 20
+GROUP = 768
+BIG = 1e30
+MESH = pl.DeviceIdType.MESH
+F32 = jnp.float32
+BF16 = jnp.bfloat16
+NN = ((1,), (0,))
+NT = ((1,), (1,))
+
+
+def dot(left, right, dims):
+    return lax.dot_general(left, right, (dims, ((), ())), preferred_element_type=F32)
+
+
+class Place:
+    def __init__(self, n_dp):
+        self.nz = n_dp // 4
+        me = lax.axis_index("dp")
+        self.core = lax.axis_index("mp")
+        self.z, self.y, self.x = me // 4, (me // 2) % 2, me % 2
+
+    def at(self, z, y, x, core):
+        return (z * 4 + y * 2 + x, core)
+
+    def over_x(self):
+        return self.at(self.z, self.y, 1 - self.x, self.core)
+
+    def over_y(self):
+        return self.at(self.z, 1 - self.y, self.x, self.core)
+
+    def over_z(self, step):
+        return self.at((self.z + step) % self.nz, self.y, self.x, self.core)
+
+    def over_core(self):
+        return self.at(self.z, self.y, self.x, 1 - self.core)
+
+    def barrier(self):
+        sem = pltpu.get_barrier_semaphore()
+        others = [self.over_core(), self.over_x(), self.over_y()]
+        others += [self.over_z(step) for step in range(1, self.nz)]
+        for other in others:
+            pl.semaphore_signal(sem, inc=1, device_id=other, device_id_type=MESH)
+        pl.semaphore_wait(sem, len(others))
+
+
+class Sender:
+    def __init__(self, send_sems, recv_sems):
+        self.send_sems, self.recv_sems = send_sems, recv_sems
+        self.count = 0
+        self.sent = []
+
+    def start(self, src, dst, device):
+        copy = pltpu.make_async_remote_copy(
+            src_ref=src,
+            dst_ref=dst,
+            send_sem=self.send_sems.at[self.count],
+            recv_sem=self.recv_sems.at[self.count],
+            device_id=device,
+            device_id_type=MESH,
+        )
+        self.count += 1
+        copy.start()
+        self.sent.append(copy)
+        return copy
+
+    def drain(self):
+        for copy in self.sent:
+            copy.wait_send()
+        self.sent = []
+
+
+class Gather:
+    def __init__(self, place, sender, weights, groups):
+        self.p, self.sender, self.weights, self.groups = place, sender, weights, groups
+        self.first, self.second, self.third = {}, {}, {}
+        self.tick_at = 0
+
+    def cut(self, k):
+        layer, low = self.groups[k]
+        return self.weights[layer], low, low + GROUP // 2, low + GROUP
+
+    def s1(self, k):
+        if k >= len(self.groups):
+            return
+        w, low, mid, high = self.cut(k)
+        p = self.p
+        own = w.at[p.z, p.y, p.x, :, low:high]
+        self.first[k] = [
+            self.sender.start(own, own, p.over_z(step)) for step in range(1, p.nz)
+        ]
+
+    def s2(self, k):
+        if k >= len(self.groups):
+            return
+        w, low, mid, high = self.cut(k)
+        p = self.p
+        for copy in self.first[k]:
+            copy.wait_recv()
+        a, b = w.at[:, p.y, p.x, :, low:mid], w.at[:, p.y, p.x, :, mid:high]
+        self.second[k] = [
+            self.sender.start(a, a, p.over_y()),
+            self.sender.start(b, b, p.over_x()),
+        ]
+
+    def s3(self, k):
+        if k < 0 or k >= len(self.groups):
+            return
+        w, low, mid, high = self.cut(k)
+        p = self.p
+        for copy in self.second[k]:
+            copy.wait_recv()
+        a, b = w.at[:, :, p.x, :, low:mid], w.at[:, p.y, :, :, mid:high]
+        self.third[k] = [
+            self.sender.start(a, a, p.over_x()),
+            self.sender.start(b, b, p.over_y()),
+        ]
+
+    def tick(self):
+        k = self.tick_at
+        if k > len(self.groups):
+            return
+        self.s2(k)
+        self.s1(k + 3)
+        self.s3(k - 1)
+        self.tick_at += 1
+
+    def ready(self, k):
+        while self.tick_at < k + 2:
+            self.tick()
+        for copy in self.third.pop(k, ()):
+            copy.wait_recv()
+
+
+class Scatter:
+    def __init__(self, place, sender, grads, groups, r1a, r1b, r2a, r2b, r3, result):
+        self.p, self.sender, self.grads, self.groups = place, sender, grads, groups
+        self.r1a, self.r1b, self.r2a, self.r2b, self.r3 = r1a, r1b, r2a, r2b, r3
+        self.result = result
+        self.first, self.second, self.third = {}, {}, {}
+        self.started = 0
+        self.tick_at = 0
+
+    def cut(self, k):
+        layer, low = self.groups[k]
+        return self.grads[layer], low, low + GROUP // 2, low + GROUP
+
+    def s1(self):
+        k = self.started
+        self.started += 1
+        g, low, mid, high = self.cut(k)
+        p = self.p
+        self.first[k] = [
+            self.sender.start(g.at[:, :, 1 - p.x, :, low:mid], self.r1a.at[k % self.r1a.shape[0]], p.over_x()),
+            self.sender.start(g.at[:, 1 - p.y, :, :, mid:high], self.r1b.at[k % self.r1b.shape[0]], p.over_y()),
+        ]
+
+    def s2(self, k):
+        g, low, mid, high = self.cut(k)
+        p = self.p
+        for copy in self.first[k]:
+            copy.wait_recv()
+        a, b = g.at[:, :, p.x, :, low:mid], g.at[:, p.y, :, :, mid:high]
+        for z in range(p.nz):
+            a[z] = (a[z].astype(F32) + self.r1a[k % self.r1a.shape[0], z].astype(F32)).astype(BF16)
+            b[z] = (b[z].astype(F32) + self.r1b[k % self.r1b.shape[0], z].astype(F32)).astype(BF16)
+        self.second[k] = [
+            self.sender.start(g.at[:, 1 - p.y, p.x, :, low:mid], self.r2a.at[k % 4], p.over_y()),
+            self.sender.start(g.at[:, p.y, 1 - p.x, :, mid:high], self.r2b.at[k % 4], p.over_x()),
+        ]
+
+    def s3(self, k):
+        g, low, mid, high = self.cut(k)
+        p = self.p
+        for copy in self.second[k]:
+            copy.wait_recv()
+        a, b = g.at[:, p.y, p.x, :, low:mid], g.at[:, p.y, p.x, :, mid:high]
+        a[...] = (a[...].astype(F32) + self.r2a[k % 4].astype(F32)).astype(BF16)
+        b[...] = (b[...].astype(F32) + self.r2b[k % 4].astype(F32)).astype(BF16)
+        self.third[k] = [
+            self.sender.start(
+                g.at[(p.z + step) % p.nz, p.y, p.x, :, low:high],
+                self.r3.at[k % 4, step - 1],
+                p.over_z(step),
+            )
+            for step in range(1, p.nz)
+        ]
+
+    def finish(self, k):
+        layer, low = self.groups[k]
+        g, low, mid, high = self.cut(k)
+        p = self.p
+        for copy in self.third[k]:
+            copy.wait_recv()
+        total = g[p.z, p.y, p.x, :, low:high].astype(F32)
+        for step in range(1, p.nz):
+            total = total + self.r3[k % 4, step - 1].astype(F32)
+        self.result[layer, :, low:high] = total
+
+    def tick(self):
+        k = self.tick_at
+        if k >= self.started + 2:
+            return
+        if k < self.started:
+            self.s2(k)
+        if 0 <= k - 1 < self.started:
+            self.s3(k - 1)
+        if 0 <= k - 2 < self.started:
+            self.finish(k - 2)
+        self.tick_at += 1
+
+
+def row_tiles(length, body):
+    def step(i, carry):
+        body(pl.ds(pl.multiple_of(i * TILE, TILE), TILE))
+        return carry
+
+    lax.fori_loop(0, length // TILE, step, 0)
+
+
+def normalised(rows):
+    centre = rows - jnp.mean(rows, axis=-1, keepdims=True)
+    spread = jnp.mean(centre * centre, axis=-1, keepdims=True)
+    rise = lax.rsqrt(spread + 1e-06)
+    return centre * rise, rise
+
+
+def encode_segments(counts, slots, qe, ke):
+    length = qe.shape[0]
+    place = lax.broadcasted_iota(jnp.int32, (length, 128), 0)
+    lane = lax.broadcasted_iota(jnp.int32, (length, 128), 1) % HEAD_DIM
+    image = jnp.zeros((length, 128), jnp.int32)
+    total = jnp.int32(0)
+    for slot in range(slots):
+        total = total + counts[slot]
+        image = image + (place >= total).astype(jnp.int32)
+    hit = image == lane
+    ke[...] = jnp.where(hit, 1.0, 0.0).astype(BF16)
+    qe[...] = jnp.where(jnp.logical_or(hit, lane > slots), 0.0, -BIG).astype(BF16)
+
+
+def attention_forward(qkv, qe, ke, log_total, mixed, between=None):
+    length, width = mixed.shape
+    lane = lax.broadcasted_iota(jnp.int32, (length, 128), 1)
+
+    def pair(at, carry):
+        low = pl.multiple_of(at * 128, 128)
+        query = qkv[:, pl.ds(low, 128)] * jnp.asarray(0.125, BF16)
+        keys = qkv[:, pl.ds(width + low, 128)]
+        values = qkv[:, pl.ds(2 * width + low, 128)].T
+        outs = []
+        for half in range(2):
+            own = (lane < HEAD_DIM) if half == 0 else (lane >= HEAD_DIM)
+            q = jnp.where(own, query, qe[...])
+            k = jnp.where(own, keys, ke[...])
+            scores = dot(k, q, NT)
+            top = jnp.max(scores, axis=0, keepdims=True)
+            raised = jnp.exp(scores - top)
+            total = jnp.sum(raised, axis=0, keepdims=True)
+            rows = slice(half * HEAD_DIM, (half + 1) * HEAD_DIM)
+            outs.append(dot(values[rows], raised.astype(BF16), NN) / total)
+            log_total[pl.ds(at * 2 + half, 1), :] = top + jnp.log(total)
+        mixed[:, pl.ds(low, 128)] = jnp.concatenate(outs, axis=0).T.astype(BF16)
+        return carry
+
+    lax.fori_loop(0, width // 128, pair, 0)
+
+
+def attention_backward(qkv, qe, ke, log_total, d_mixed):
+    length, width = d_mixed.shape
+    lane = lax.broadcasted_iota(jnp.int32, (length, 128), 1)
+
+    def pair(at, carry):
+        low = pl.multiple_of(at * 128, 128)
+        query = qkv[:, pl.ds(low, 128)] * jnp.asarray(0.125, BF16)
+        keys = qkv[:, pl.ds(width + low, 128)]
+        values = qkv[:, pl.ds(2 * width + low, 128)]
+        d_out = d_mixed[:, pl.ds(low, 128)]
+        keys_t = keys.T
+        d_query, d_keys, d_values = [], [], []
+        for half in range(2):
+            own = (lane < HEAD_DIM) if half == 0 else (lane >= HEAD_DIM)
+            q = jnp.where(own, query, qe[...])
+            k = jnp.where(own, keys, ke[...])
+            v = jnp.where(own, values, jnp.zeros_like(values))
+            probs = jnp.exp(dot(k, q, NT) - log_total[pl.ds(at * 2 + half, 1), :])
+            d_probs = dot(v, d_out, NT)
+            mean = jnp.sum(probs * d_probs, axis=0, keepdims=True)
+            d_scores = (probs * (d_probs - mean)).astype(BF16)
+            d_values.append(dot(probs.astype(BF16), d_out, NN))
+            d_keys.append(dot(d_scores, query, NN))
+            rows = slice(half * HEAD_DIM, (half + 1) * HEAD_DIM)
+            d_query.append(dot(keys_t[rows], d_scores, NN))
+        first = lane < HEAD_DIM
+        d_q = jnp.concatenate(d_query, axis=0).T * 0.125
+        qkv[:, pl.ds(low, 128)] = d_q.astype(BF16)
+        qkv[:, pl.ds(width + low, 128)] = jnp.where(first, *d_keys).astype(BF16)
+        qkv[:, pl.ds(2 * width + low, 128)] = jnp.where(first, *d_values).astype(BF16)
+        return carry
+
+    lax.fori_loop(0, width // 128, pair, 0)
+
+
+class Exchange:
+    def __init__(self, place, sender, out, into):
+        self.p, self.sender, self.out, self.into = place, sender, out, into
+        self.turn = 0
+        self.copies = {}
+        length = out.shape[1]
+        cut = (length // TILE + 1) // 2 * TILE
+        self.chunks = ((0, cut), (cut, length))
+
+    def send(self, compute):
+        slot = self.turn % 2
+        for copy in self.copies.get(slot, ()):
+            copy.wait_send()
+            self.sender.sent = [item for item in self.sender.sent if item is not copy]
+        self.copies[slot] = []
+        for low, high in self.chunks:
+            self.out[slot, low:high, :] = compute(low, high).astype(BF16)
+            piece = self.out.at[slot, low:high, :]
+            self.copies[slot].append(
+                self.sender.start(piece, self.into.at[slot, low:high, :], self.p.over_core())
+            )
+
+    def take(self, body):
+        slot = self.turn % 2
+        self.turn += 1
+        for (low, high), copy in zip(self.chunks, self.copies[slot]):
+            copy.wait_recv()
+
+            def step(i, carry, low=low):
+                rows = pl.ds(pl.multiple_of(low + i * TILE, TILE), TILE)
+                total = self.out[slot, rows, :].astype(F32) + self.into[slot, rows, :].astype(F32)
+                body(rows, total)
+                return carry
+
+            lax.fori_loop(0, (high - low) // TILE, step, 0)
+
+
+def flat(w, low, high):
+    value = w[:, :, :, :, low:high]
+    return value.reshape(-1, high - low)
+
+
+def gelu_and_slope(hidden):
+    cdf = 0.5 * (1.0 + lax.erf(hidden * (0.5**0.5)))
+    slope = cdf + hidden * (jnp.exp(-0.5 * hidden * hidden) * 0.3989422804014327)
+    return hidden * cdf, slope
+
+
+def forward_kernel(
+    n_dp, cuts, slots,
+    counts, patches, pieces, norms,
+    o_weights, o_rows, o_middle, o_normed_a, o_qkv, o_mixed, o_normed_b, o_active, o_slope, o_log,
+    o_result,
+    w0, w1, rows, middle, normed_a, qkv, mixed, normed_b, active, slope, log_total, final,
+    x_out, x_in, qe, ke, send_sems, recv_sems, local_sems,
+):
+    layers, half = 2, patches.shape[0]
+    length = 2 * half
+    c_qkv, c_out, c_up, c_down = cuts
+    p = Place(n_dp)
+    sender = Sender(send_sems, recv_sems)
+    local = []
+
+    def move(src, dst):
+        copy = pltpu.make_async_copy(src, dst, local_sems.at[len(local)])
+        copy.start()
+        local.append(copy)
+        return copy
+
+    weights = (w0, w1)
+    loads = [move(pieces.at[l], weights[l].at[p.z, p.y, p.x]) for l in range(layers)]
+    p.barrier()
+    groups = [(l, low) for l in range(layers) for low in range(0, c_down[1], GROUP)]
+    per = len(groups) // layers
+    gather = Gather(p, sender, weights, groups)
+    loads[0].wait()
+    gather.s1(0)
+    gather.s1(1)
+    own_rows = pl.ds(pl.multiple_of(p.core * half, half), half)
+    rows[0, own_rows, :] = patches[...].astype(F32)
+    swap = sender.start(rows.at[0, own_rows, :], rows.at[0, own_rows, :], p.over_core())
+    loads[1].wait()
+    gather.s1(2)
+    encode_segments(counts, slots, qe, ke)
+    swap.wait_recv()
+    exchange = Exchange(p, sender, x_out, x_in)
+
+    def norm_into(target, layer, which, at, value):
+        hat, _ = normalised(value)
+        gain, shift = norms[layer, which : which + 1, :], norms[layer, which + 1 : which + 2, :]
+        target[layer, at, :] = (hat * gain + shift).astype(BF16)
+
+    row_tiles(length, lambda at: norm_into(normed_a, 0, 0, at, rows[0, at, :]))
+    saves = [(rows, o_rows, 0), (normed_a, o_normed_a, 0)]
+
+    def save(*items):
+        for src, dst, layer in items:
+            move(src.at[layer], dst.at[layer])
+
+    save(*saves)
+    for layer in range(layers):
+        w, base = weights[layer], per * layer
+        qkv_end = c_qkv[1]
+        for k in range(-(-qkv_end // GROUP)):
+            gather.ready(base + k)
+            low, high = k * GROUP, min(qkv_end, (k + 1) * GROUP)
+            qkv[layer, :, low:high] = dot(normed_a[layer], flat(w, low, high), NN).astype(BF16)
+        gather.tick()
+        attention_forward(qkv.at[layer], qe, ke, log_total.at[layer], mixed.at[layer])
+        save((qkv, o_qkv, layer), (log_total, o_log, layer), (mixed, o_mixed, layer))
+        gather.ready(base + (c_out[1] - 1) // GROUP)
+        w_out = flat(w, *c_out)
+        exchange.send(lambda low, high: dot(mixed[layer, low:high, :], w_out, NT))
+        gather.tick()
+
+        def mid_step(at, total):
+            value = rows[layer, at, :] + total
+            middle[layer, at, :] = value
+            norm_into(normed_b, layer, 2, at, value)
+
+        exchange.take(mid_step)
+        save((middle, o_middle, layer), (normed_b, o_normed_b, layer))
+        for k in range(c_up[0] // GROUP, c_up[1] // GROUP):
+            gather.ready(base + k)
+            low = k * GROUP - c_up[0]
+            for at in range(0, GROUP, GROUP // 2):
+                cols = slice(low + at, low + at + GROUP // 2)
+                first = k * GROUP + at
+                hidden = dot(normed_b[layer], flat(w, first, first + GROUP // 2), NN)
+                act, rise = gelu_and_slope(hidden)
+                active[layer, :, cols] = act.astype(BF16)
+                slope[layer, :, cols] = rise.astype(BF16)
+        save((active, o_active, layer), (slope, o_slope, layer))
+        gather.tick()
+        for k in range(c_down[0] // GROUP, c_down[1] // GROUP):
+            gather.ready(base + k)
+        if True:
+            w_down = flat(w, *c_down)
+            exchange.send(lambda low, high: dot(active[layer, low:high, :], w_down, NT))
+        move(w, o_weights.at[layer])
+        gather.tick()
+        if layer + 1 < layers:
+
+            def next_step(at, total):
+                value = middle[layer, at, :] + total
+                rows[layer + 1, at, :] = value
+                norm_into(normed_a, layer + 1, 0, at, value)
+
+            exchange.take(next_step)
+            save((rows, o_rows, layer + 1), (normed_a, o_normed_a, layer + 1))
+        else:
+
+            def last_step(at, total):
+                final[at, :] = middle[layer, at, :] + total
+
+            exchange.take(last_step)
+    o_result[...] = final[own_rows, :].astype(BF16)
+    sender.drain()
+    for copy in local[layers:]:
+        copy.wait()
+
+
+def backward_kernel(
+    n_dp, cuts, slots,
+    counts, cotangent, norms,
+    i_weights, i_rows, i_middle, i_normed_a, i_qkv, i_mixed, i_normed_b, i_active, i_slope, i_log,
+    o_input, o_pieces, o_norms,
+    g0, g1, r1a, r1b, r2a, r2b, r3,
+    w, kept, normed_a, qkv, mixed, normed_b, active, slope, log_total,
+    grad, rounded, turned, x_out, x_in, qe, ke, send_sems, recv_sems, local_sems,
+):
+    layers, half = 2, cotangent.shape[0]
+    length = 2 * half
+    c_qkv, c_out, c_up, c_down = cuts
+    p = Place(n_dp)
+    sender = Sender(send_sems, recv_sems)
+    count = [0]
+
+    def load(src, dst):
+        copy = pltpu.make_async_copy(src, dst, local_sems.at[count[0]])
+        count[0] += 1
+        copy.start()
+        return copy
+
+    def load_mlp(l):
+        cols = slice(c_up[0], c_down[1])
+        return dict(
+            active=load(i_active.at[l], active),
+            slope=load(i_slope.at[l], slope),
+            weights=load(i_weights.at[l, :, :, :, :, cols], w.at[:, :, :, :, cols]),
+            normed_b=load(i_normed_b.at[l], normed_b),
+            middle=load(i_middle.at[l], kept),
+        )
+
+    def load_attention(l):
+        cols = slice(c_qkv[0], c_out[1])
+        return dict(
+            mixed=load(i_mixed.at[l], mixed),
+            weights=load(i_weights.at[l, :, :, :, :, cols], w.at[:, :, :, :, cols]),
+            qkv=load(i_qkv.at[l], qkv),
+            log=load(i_log.at[l], log_total),
+            normed_a=load(i_normed_a.at[l], normed_a),
+        )
+
+    mlp = load_mlp(layers - 1)
+    att = load_attention(layers - 1)
+    p.barrier()
+    own_rows = pl.ds(pl.multiple_of(p.core * half, half), half)
+    total = jnp.int32(0)
+    for slot in range(slots):
+        total = total + counts[slot]
+    place = lax.broadcasted_iota(jnp.int32, (half, 1), 0) + p.core * half
+    grad[own_rows, :] = jnp.where(place < total, cotangent[...].astype(F32), 0.0)
+    swap = sender.start(grad.at[own_rows, :], grad.at[own_rows, :], p.over_core())
+    encode_segments(counts, slots, qe, ke)
+    o_norms[...] = jnp.zeros_like(o_norms)
+    exchange = Exchange(p, sender, x_out, x_in)
+    grads = (g0, g1)
+    per = c_down[1] // GROUP
+    order = [k for k in range(c_down[0] // GROUP, per)]
+    order += [k for k in range(c_up[0] // GROUP, c_up[1] // GROUP)]
+    order += [k for k in reversed(range(0, c_up[0] // GROUP))]
+    groups = [(l, k * GROUP) for l in reversed(range(layers)) for k in order]
+    scatter = Scatter(p, sender, grads, groups, r1a, r1b, r2a, r2b, r3, o_pieces)
+    swap.wait_recv()
+    sender.drain()
+
+    def store(layer, low, value):
+        g = grads[layer]
+        shape = g.shape[:4] + (value.shape[1],)
+        g[:, :, :, :, low : low + value.shape[1]] = value.astype(BF16).reshape(shape)
+
+    def norm_step(layer, which, at, total):
+        hat, rise = normalised(kept[at, :])
+        o_norms[layer, which : which + 1, :] += jnp.sum(total * hat, axis=0, keepdims=True)
+        o_norms[layer, which + 1 : which + 2, :] += jnp.sum(total, axis=0, keepdims=True)
+        d_hat = total * norms[layer, which : which + 1, :]
+        flat_mean = jnp.mean(d_hat, axis=-1, keepdims=True)
+        hat_mean = jnp.mean(d_hat * hat, axis=-1, keepdims=True)
+        value = grad[at, :] + rise * (d_hat - flat_mean - hat * hat_mean)
+        grad[at, :] = value
+        rounded[at, :] = value.astype(BF16)
+
+    def round_step(at):
+        rounded[at, :] = grad[at, :].astype(BF16)
+
+    row_tiles(length, round_step)
+    for layer in reversed(range(layers)):
+        turned[...] = rounded[...].T
+        mlp["active"].wait()
+        for k in range(c_down[0] // GROUP, c_down[1] // GROUP):
+            low = k * GROUP - c_down[0]
+            store(layer, k * GROUP, dot(turned[...], active[:, low : low + GROUP], NN))
+            scatter.s1()
+        mlp["weights"].wait()
+        mlp["slope"].wait()
+        step = GROUP // 2
+        for at in range(0, c_down[1] - c_down[0], step):
+            cols = slice(at, at + step)
+            first = c_down[0] + at
+            d_active = dot(rounded[...], flat(w, first, first + step), NN)
+            slope[:, cols] = (d_active * slope[:, cols].astype(F32)).astype(BF16)
+        scatter.tick()
+        mlp["normed_b"].wait()
+        turned[...] = normed_b[...].T
+        for k in range(c_up[0] // GROUP, c_up[1] // GROUP):
+            low = k * GROUP - c_up[0]
+            store(layer, k * GROUP, dot(turned[...], slope[:, low : low + GROUP], NN))
+            scatter.s1()
+        w_up = flat(w, *c_up)
+        exchange.send(lambda low, high: dot(slope[low:high, :], w_up, NT))
+        scatter.tick()
+        mlp["middle"].wait()
+        exchange.take(lambda at, total: norm_step(layer, 2, at, total))
+        rows_load = load(i_rows.at[layer], kept)
+        if layer:
+            mlp = load_mlp_next(load, layer - 1, i_active, i_slope, i_weights, i_normed_b,
+                                active, slope, w, normed_b, slice(c_up[0], c_down[1]))
+        turned[...] = rounded[...].T
+        att["mixed"].wait()
+        store(layer, c_out[0], dot(turned[...], mixed[...], NN))
+        att["weights"].wait()
+        mixed[...] = dot(rounded[...], flat(w, *c_out), NN).astype(BF16)
+        scatter.tick()
+        att["qkv"].wait()
+        att["log"].wait()
+        attention_backward(qkv, qe, ke, log_total, mixed)
+        att["normed_a"].wait()
+        turned[...] = normed_a[...].T
+        for k in reversed(range(0, c_out[1] // GROUP)):
+            low, high = k * GROUP, min(c_qkv[1], (k + 1) * GROUP)
+            store(layer, low, dot(turned[...], qkv[:, low:high], NN))
+            scatter.s1()
+        w_qkv = flat(w, *c_qkv)
+        exchange.send(lambda low, high: dot(qkv[low:high, :], w_qkv, NT))
+        scatter.tick()
+        rows_load.wait()
+        exchange.take(lambda at, total: norm_step(layer, 0, at, total))
+        if layer:
+            mlp["middle"] = load(i_middle.at[layer - 1], kept)
+            att = load_attention(layer - 1)
+        scatter.tick()
+    o_input[...] = grad[own_rows, :]
+    while scatter.tick_at < len(groups) + 2:
+        scatter.tick()
+    sender.drain()
+
+
+def load_mlp_next(load, l, i_active, i_slope, i_weights, i_normed_b, active, slope, w, normed_b, cols):
+    return dict(
+        active=load(i_active.at[l], active),
+        slope=load(i_slope.at[l], slope),
+        weights=load(i_weights.at[l, :, :, :, :, cols], w.at[:, :, :, :, cols]),
+        normed_b=load(i_normed_b.at[l], normed_b),
+    )
+
+
+def passes_by_xla(
     patches,
     cotangent,
     patch_counts,
@@ -91,15 +715,6 @@
     up_weight,
     down_weight,
     norms,
-    qkv_rows,
-    qkv_cols,
-    out_rows,
-    out_cols,
-    up_rows,
-    up_cols,
-    down_rows,
-    down_cols,
-    norm_state,
 ):
     layers = qkv_weight.shape[0]
     half = patches.shape[0]
@@ -237,8 +852,153 @@
             lax.psum_scatter(g_out, "dp", scatter_dimension=1, tiled=True),
             lax.psum_scatter(g_up, "dp", scatter_dimension=0, tiled=True),
             lax.psum_scatter(g_down, "dp", scatter_dimension=1, tiled=True),
-            lax.psum_scatter(norm_terms, "dp", scatter_dimension=1, tiled=True),
-        )
+            lax.psum(norm_terms, "mp"),
+        )
+    return activations, grad, [item[:4] for item in reduced], jnp.stack([item[4] for item in reduced])
+
+
+def passes_by_kernels(
+    patches,
+    cotangent,
+    patch_counts,
+    qkv_weight,
+    out_weight,
+    up_weight,
+    down_weight,
+    norms,
+):
+    layers, depth, _, local = qkv_weight.shape
+    n_dp = lax.axis_size("dp")
+    nz, half, wide = n_dp // 4, patches.shape[0], up_weight.shape[2]
+    length, slots = 2 * half, patch_counts.shape[0]
+    ends = [0, 3 * local, 4 * local, 4 * local + wide, 4 * local + 2 * wide]
+    cuts = tuple(zip(ends[:-1], ends[1:]))
+    columns, n_groups = ends[-1], layers * ends[-1] // GROUP
+    pieces = jnp.concatenate(
+        [
+            qkv_weight.reshape(layers, depth, 3 * local),
+            out_weight.transpose(0, 2, 1),
+            up_weight,
+            down_weight.transpose(0, 2, 1),
+        ],
+        axis=2,
+    ).astype(BF16)
+    vmem, smem, hbm = [
+        pl.BlockSpec(memory_space=space) for space in (pltpu.VMEM, pltpu.SMEM, pl.ANY)
+    ]
+    shape = jax.ShapeDtypeStruct
+    whole = (nz, 2, 2, depth, columns)
+    rows_f32, rows_bf16 = ((length, D), F32), ((length, D), BF16)
+    kept = [
+        rows_f32,
+        rows_f32,
+        rows_bf16,
+        ((length, 3 * local), BF16),
+        ((length, local), BF16),
+        rows_bf16,
+        ((length, wide), BF16),
+        ((length, wide), BF16),
+        ((8, length), F32),
+    ]
+    saved = [shape((layers,) + dims, kind) for dims, kind in kept]
+    sems = [
+        pltpu.SemaphoreType.DMA((96,)),
+        pltpu.SemaphoreType.DMA((96,)),
+        pltpu.SemaphoreType.DMA((32,)),
+    ]
+    codes = [pltpu.VMEM((length, 128), BF16)] * 2
+    swaps = [pltpu.VMEM((2, length, D), BF16)] * 2
+    outs = pl.pallas_call(
+        functools.partial(forward_kernel, n_dp, cuts, slots),
+        out_shape=[shape((layers,) + whole, BF16)] + saved + [shape((half, D), BF16)],
+        in_specs=[smem, vmem, hbm, vmem],
+        out_specs=[hbm] * (1 + len(saved)) + [vmem],
+        scratch_shapes=[pltpu.VMEM(whole, BF16)] * layers
+        + [pltpu.VMEM((layers,) + dims, kind) for dims, kind in kept]
+        + [pltpu.VMEM((length, D), F32)]
+        + swaps
+        + codes
+        + sems,
+        compiler_params=pltpu.CompilerParams(
+            collective_id=0, has_side_effects=True, vmem_limit_bytes=VMEM_BYTES
+        ),
+        name="forward",
+    )(patch_counts, patches, pieces, norms)
+    saved, activations = outs[:-1], outs[-1]
+    own = (nz, 2, depth, GROUP // 2)
+    grad, sums, norm_terms = pl.pallas_call(
+        functools.partial(backward_kernel, n_dp, cuts, slots),
+        out_shape=[
+            shape((half, D), F32),
+            shape((layers, depth, columns), F32),
+            shape((layers, 4, D), F32),
+        ],
+        in_specs=[smem, vmem, vmem] + [hbm] * len(saved),
+        out_specs=[vmem, vmem, vmem],
+        scratch_shapes=[pltpu.VMEM(whole, BF16)] * layers
+        + [pltpu.VMEM((n_groups // 2,) + own, BF16)] * 2
+        + [pltpu.VMEM((4, nz, depth, GROUP // 2), BF16)] * 2
+        + [pltpu.VMEM((4, nz - 1, depth, GROUP), BF16)]
+        + [pltpu.VMEM(whole, BF16)]
+        + [pltpu.VMEM(dims, kind) for dims, kind in kept[1:]]
+        + [
+            pltpu.VMEM((length, D), F32),
+            pltpu.VMEM((length, D), BF16),
+            pltpu.VMEM((D, length), BF16),
+        ]
+        + swaps
+        + codes
+        + sems,
+        compiler_params=pltpu.CompilerParams(
+            collective_id=1, has_side_effects=True, vmem_limit_bytes=VMEM_BYTES
+        ),
+        name="backward",
+    )(patch_counts, cotangent, norms, *saved)
+    reduced = []
+    for layer in range(layers):
+        parts = [sums[layer, :, low:high] for low, high in cuts]
+        reduced.append(
+            (parts[0].reshape(depth, 3, local), parts[1].T, parts[2], parts[3].T)
+        )
+    return activations, grad, reduced, norm_terms
+
+
+def kernels_fit(patches, qkv_weight):
+    length = 2 * patches.shape[0]
+    depth, local = qkv_weight.shape[1], qkv_weight.shape[3]
+    return (
+        lax.axis_size("mp") == 2
+        and lax.axis_size("dp") % 4 == 0
+        and depth % 16 == 0
+        and length % TILE == 0
+        and (4 * local) % GROUP == 0
+    )
+
+
+def per_device(
+    patches,
+    cotangent,
+    patch_counts,
+    qkv_weight,
+    out_weight,
+    up_weight,
+    down_weight,
+    norms,
+    qkv_rows,
+    qkv_cols,
+    out_rows,
+    out_cols,
+    up_rows,
+    up_cols,
+    down_rows,
+    down_cols,
+    norm_state,
+):
+    layers = qkv_weight.shape[0]
+    passes = passes_by_kernels if kernels_fit(patches, qkv_weight) else passes_by_xla
+    activations, grad, reduced, norm_terms = passes(
+        patches, cotangent, patch_counts, qkv_weight, out_weight, up_weight, down_weight, norms
+    )
     col_axes = ("mp", "dp", "mp", "dp")
     row_counts = (D, D, D, FF)
     col_counts = (3 * D, D, FF, D)
@@ -249,7 +1009,6 @@
     grads = [reduced[layer][which] for layer, which in entries]
     row_olds = [row_states[which][layer] for layer, which in entries]
     col_olds = [col_states[which][layer] for layer, which in entries]
-    norm_partial = jnp.stack([reduced[layer][4] for layer in range(layers)])
     width = norm_state.shape[2]
     row_parts, col_parts = ([], [])
     for position, (layer, which) in enumerate(entries):
@@ -262,19 +1021,20 @@
             row_parts[position] if col_axes[which] == "mp" else col_parts[position]
             for position, (layer, which) in enumerate(entries)
         ]
-        + [norm_partial]
     )
     data_side = tuple(
         (
             col_parts[position] if col_axes[which] == "mp" else row_parts[position]
             for position, (layer, which) in enumerate(entries)
         )
-    )
+    ) + (norm_terms,)
     model_sums = jax.tree.map(
         lambda part: part.astype(jnp.float32), lax.psum(for_sending(model_side), "mp")
     )
     data_sums = lax.psum(data_side, "dp")
-    norm_grad = model_sums[len(entries)]
+    norm_grad = lax.dynamic_slice_in_dim(
+        data_sums[len(entries)], lax.axis_index("dp") * width, width, 2
+    )
     row_sums = [
         model_sums[position] if col_axes[which] == "mp" else data_sums[position]
         for position, (layer, which) in enumerate(entries)

time: 2370 us -> 587 us (0.25)
  waiting for transfers between devices: 1670 us -> 0 us
  Pallas kernels: 0 us -> 331 us
  matrix products: 220 us -> 0 us
  blocking collectives: 252 us -> 162 us
  other arithmetic: 117 us -> 35.2 us
  local copies, waits for them, and re-layouts: 57.1 us -> 26.4 us
    reduce_scatter x16 -> x0, waiting for transfers between devices: 1090 us -> none  [the longest x2 284 us: per_device(): lax.psum_scatter(g_down, 'dp', scatter_dimension=1, tiled=True)]
    all_gather x14 -> x0, waiting for transfers between devices: 337 us -> none  [the longest x2 123 us: per_device(): lax.all_gather(pieces[2], 'dp', axis=0, tiled=True)]
    pallas_call x0 -> x2, Pallas kernels: none -> 331 us  [the longest x1 181 us: passes_by_kernels(): pl.pallas_call(functools.partial(backward_kernel, n_dp, cuts, slots), out...]
    unnamed x34 -> x0, waiting for transfers between devices: 246 us -> none
    dot_general x36 -> x0, matrix products: 220 us -> none  [the longest x2 28.6 us: attend_back(): jnp.einsum('qhd,khd->hqk', grad_mixed, values, preferred_element_type=jnp...]
    all_gather x2 -> x0, blocking collectives: 96.4 us -> none  [per_device(): lax.all_gather(pieces[1], 'dp', axis=1, tiled=True)]
    reduce_sum x19 -> x0, other arithmetic: 37 us -> none  [the longest x2 16.2 us: attend(): total = jnp.sum(raised, axis=-1, keepdims=True)]
    convert_element_type x14 -> x0, other arithmetic: 32.6 us -> none  [the longest x2 15.6 us: attend_back(): (probs * (d_probs - jnp.sum(probs * d_probs, axis=-1, keepdims=True))).as...]
  transfers between devices with their start and end apart: 32 -> 0, of which waited for: 30 -> 0; matrix products, arithmetic and copies ran while one was open for 6% -> 0% of each run, Pallas kernels for 0% -> 0%
where the time goes in v1:
time: 587 us; the launch traced here: 577 us
  Pallas kernels  331 us (56%)
  blocking collectives  162 us (28%)
  other arithmetic  35.2 us (6%)
  local copies, waits for them, and re-layouts  26.4 us (4%)
  between operations  23 us (4%)
    pallas_call x1, Pallas kernels, passes_by_kernels(): pl.pallas_call(functools.partial(backward_kernel, n_dp, cuts, slots), out...  181 us
    pallas_call x1, Pallas kernels, passes_by_kernels(): pl.pallas_call(functools.partial(forward_kernel, n_dp, cuts, slots), out_...  150 us
    psum x1, blocking collectives, per_device(): data_sums = lax.psum(data_side, 'dp')  78.1 us
    psum x1, blocking collectives, per_device(): lax.psum((step_all, jnp.stack(weight_parts)), ('dp', 'mp'))  41.3 us
    psum x1, blocking collectives, per_device(): row_totals = lax.psum(shares, ('dp', 'mp'))  36.8 us

profile of v1, /device:TPU:0, one launch (start us, length us, event | category | flops | bytes accessed | tf_op | source)
XLA Modules:
  0.0 577.3 jit_solution(15801071750188673773)
XLA Ops:
  0.7 1.2 convert_bitcast_fusion
  1.9 1.1 convert.17
  3.1 1.0 pad_maximum_fusion.pieces
  4.0 150.2 %forward.1 = (bf16[2,4,2,2,48,4608]{5,4,3,2,1,0:T(8,128)(2,1)}, f32[2,784,768]{2,1,0:T(8,128)}, f32[2,784,768]{2,1,0:T(8,128)}, bf16[2,784,768]{2,1,0:T(8,128)(2...) custom-call(s32[4]{0:T(128)} %counts.3, ...), custom_call_target="tpu_custom_call" | custom-call | tf_op jit(solution)/shard_map/forward/pallas_call | solution.py:911
  154.2 180.7 %backward.1 = (f32[392,768]{1,0:T(8,128)}, f32[2,48,4608]{2,1,0:T(8,128)}, f32[2,4,768]{2,1,0:T(4,128)}) custom-call(s32[4]{0:T(128)} %counts.3, bf16[392,768]{1,0:T(8,128)(2,1)} %cotangent.1, f32[2,4,768]{2,1,0:T(4,128)} %norms.3, bf16[2,4,2,2,48,4608]{5,4,3,2,1,0:T(8,128)(2,1)} %get-tuple-element.42.i_weights, f32[2,784,768]{2,1,0:T(8,128)} %get-tuple-element.43.i_rows, ...), custom_call_target="tpu_custom_call" | custom-call | tf_op jit(solution)/shard_map/backward/pallas_call | solution.py:929
  335.0 1.1 fusion.58
  338.5 0.9 stack.197
  340.0 78.1 %all-reduce.1 = (f32[2,4,768]{2,1,0:T(4,128)S(1)}, f32[384]{0:T(512)S(1)}, f32[1536]{0:T(1024)S(1)}, f32[384]{0:T(512)S(1)}, f32[1536]{0:T(1024)S(1)}, /*index=5...) all-reduce(f32[2,4,768]{2,1,0:T(4,128)S(1)} %copy-done.28, ...), channel_id=1, replica_groups=mesh['dp'=16,'mp'=2] {'dp'}, use_global_device_ids=true, to_apply=%region_0.0 | all-reduce | flops 15360 | bytes 122880 | tf_op jit(solution)/shard_map/psum | solution.py:1034
  419.4 2.4 all-reduce.3
  421.9 1.2 fusion.51
  425.8 1.2 fusion.50
  430.3 36.8 %psum.151 = f32[8]{0:T(128)S(1)} all-reduce(f32[8]{0:T(128)S(1)} %stack.218), channel_id=1, replica_groups=mesh['dp'=16,'mp'=2] {'dp','mp'}, use_global_device_ids=true, to_apply=%region_36.0 | all-reduce | flops 8 | bytes 64 | tf_op jit(solution)/shard_map/psum | solution.py:1056
  473.6 3.1 all-reduce.2
  478.7 0.8 multiply_reduce_fusion.7
  481.0 1.6 fusion.5
  484.4 1.5 multiply_reduce_fusion.1
  485.9 5.8 %stack.227 = f32[8]{0:T(128)} concatenate(f32[1]{0:T(128)} %bitcast.49, f32[1]{0:T(128)} %bitcast.52, f32[1]{0:T(128)} %bitcast.54, f32[1]{0:T(128)} %bitcast.57, f32[1]{0:T(128)} %bitcast.60, f32[1]{0:T(128)} %bitcast.63, f32[1]{0:T(128)} %bitcast.65, f32[1]{0:T(128)} %bitcast.68), dimensions={0} | concatenate | bytes 64 | tf_op jit(solution)/shard_map/stack | solution.py:1080
  491.7 1.3 reshape.426
  492.9 1.3 pad_maximum_fusion.12
  494.3 1.1 fusion.59
  496.0 0.9 fusion
  496.9 1.5 fusion.34
  499.9 5.8 stack.209
  505.6 41.3 %all-reduce = (f32[2,8]{1,0:T(2,128)}, f32[8]{0:T(128)}) all-reduce(f32[2,8]{1,0:T(2,128)} %pad_maximum_fusion.12, f32[8]{0:T(128)} %stack.209), channel_id=1, replica_groups=mesh['dp'=16,'mp'=2] {'dp','mp'}, use_global_device_ids=true, to_apply=%region_60.0 | all-reduce | flops 24 | bytes 192 | tf_op jit(solution)/shard_map/psum | solution.py:1082
  547.0 0.8 multiply_sqrt_fusion.1
  549.1 1.6 fusion.63
  552.9 1.0 multiply_subtract_fusion.1
  553.9 0.9 pad_maximum_fusion.2
  562.5 1.0 fusion.48
  566.4 1.0 fusion.47
  575.1 0.8 copy.87
  575.9 1.0 copy.88
  (170 shorter events, 24.4 us)
Async XLA Ops:
  337.7 80.4 %copy-start.20 = (f32[2,4,48]{2,1,0:T(4,128)S(1)}, f32[2,4,48]{2,1,0:T(4,128)}, u32[]{:S(2)}) copy-start(f32[2,4,48]{2,1,0:T(4,128)} %param.34) | copy-start | bytes 4612
  337.7 84.1 %copy-start.47 = (f32[2,48]{1,0:T(2,128)S(1)}, f32[2,48]{1,0:T(2,128)}, u32[]{:S(2)}) copy-start(f32[2,48]{1,0:T(2,128)} %param.30) | copy-start | bytes 1156
  337.7 84.1 %copy-start.48 = (f32[2,48]{1,0:T(2,128)S(1)}, f32[2,48]{1,0:T(2,128)}, u32[]{:S(2)}) copy-start(f32[2,48]{1,0:T(2,128)} %param.26) | copy-start | bytes 1156
  337.8 86.0 %copy-start.46 = (f32[2,384]{1,0:T(2,128)S(1)}, f32[2,384]{1,0:T(2,128)}, u32[]{:S(2)}) copy-start(f32[2,384]{1,0:T(2,128)} %param.28) | copy-start | bytes 9220
  337.8 87.9 %copy-start.30 = (f32[2,1536]{1,0:T(2,128)S(1)}, f32[2,1536]{1,0:T(2,128)}, u32[]{:S(2)}) copy-start(f32[2,1536]{1,0:T(2,128)} %param.32) | copy-start | bytes 36868
  337.8 130.6 %copy-start.31 = (f32[2,3,384]{2,0,1:T(2,128)S(1)}, f32[2,3,384]{2,0,1:T(2,128)}, u32[]{:S(2)}) copy-start(f32[2,3,384]{2,0,1:T(2,128)} %param.27) | copy-start | bytes 27652
  338.5 132.8 %copy-start.49 = (f32[2,48]{1,0:T(2,128)S(1)}, f32[2,48]{1,0:T(2,128)}, u32[]{:S(2)}) copy-start(f32[2,48]{1,0:T(2,128)} %param.29) | copy-start | bytes 1156
  338.5 132.9 %copy-start.50 = (f32[2,48]{1,0:T(2,128)S(1)}, f32[2,48]{1,0:T(2,128)}, u32[]{:S(2)}) copy-start(f32[2,48]{1,0:T(2,128)} %param.33) | copy-start | bytes 1156
  418.8 49.7 %copy-start.22 = (f32[2,4,48]{2,1,0:T(4,128)}, f32[2,4,48]{2,1,0:T(4,128)S(1)}, u32[]{:S(2)}) copy-start(f32[2,4,48]{2,1,0:T(4,128)S(1)} %get-tuple-element.255) | copy-start | bytes 4612
  423.1 49.6 %copy-start.34 = (f32[48]{0:T(128)}, f32[48]{0:T(128)S(1)}, u32[]{:S(2)}) copy-start(f32[48]{0:T(128)S(1)} %get-tuple-element.215) | copy-start | bytes 580
  423.1 49.6 %copy-start.36 = (f32[48]{0:T(128)}, f32[48]{0:T(128)S(1)}, u32[]{:S(2)}) copy-start(f32[48]{0:T(128)S(1)} %get-tuple-element.217) | copy-start | bytes 580
  424.4 48.3 %copy-start.24 = (f32[384]{0:T(512)}, f32[384]{0:T(512)S(1)}, u32[]{:S(2)}) copy-start(f32[384]{0:T(512)S(1)} %get-tuple-element.148) | copy-start | bytes 4612
  424.4 55.2 %copy-start.26 = (f32[384]{0:T(512)}, f32[384]{0:T(512)S(1)}, u32[]{:S(2)}) copy-start(f32[384]{0:T(512)S(1)} %get-tuple-element.213) | copy-start | bytes 4612
  470.0 28.5 %copy-start.2 = (f32[2,48,1536]{2,1,0:T(8,128)S(1)}, f32[2,48,1536]{2,1,0:T(8,128)}, u32[]{:S(2)}) copy-start(f32[2,48,1536]{2,1,0:T(8,128)} %param.23) | copy-start | bytes 1769476
  472.8 26.3 %copy-start.1 = (f32[2,1536,48]{1,2,0:T(8,128)S(1)}, f32[2,1536,48]{1,2,0:T(8,128)}, u32[]{:S(2)}) copy-start(f32[2,1536,48]{1,2,0:T(8,128)} %param.24) | copy-start | bytes 1769476
  552.9 4.9 copy-start.4
  552.9 4.9 copy-start.19
  552.9 4.9 copy-start.35
  556.1 5.5 copy-start.9
  556.1 5.5 copy-start.25
  556.1 5.5 copy-start.27
  556.1 5.5 copy-start.41
  556.2 5.5 copy-start.43
  558.1 8.0 %copy-start.15 = (f32[1536]{0:T(1024)S(1)}, f32[1536]{0:T(1024)}, u32[]{:S(2)}) copy-start(f32[1536]{0:T(1024)} %get-tuple-element.211) | copy-start | bytes 18436
  558.1 8.0 %copy-start.39 = (f32[48]{0:T(128)S(1)}, f32[48]{0:T(128)}, u32[]{:S(2)}) copy-start(f32[48]{0:T(128)} %copy-done.38) | copy-start | bytes 580
  558.2 8.0 %copy-start.45 = (f32[48]{0:T(128)S(1)}, f32[48]{0:T(128)}, u32[]{:S(2)}) copy-start(f32[48]{0:T(128)} %copy-done.44) | copy-start | bytes 580
  566.3 5.1 copy-start.32
  566.4 5.1 copy-start.33
  566.4 5.6 copy-start.14
  566.4 7.5 %copy-start.29 = (f32[2,4,48]{2,1,0:T(4,128)S(1)}, f32[2,4,48]{2,1,0:T(4,128)}, u32[]{:S(2)}) copy-start(f32[2,4,48]{2,1,0:T(4,128)} %get-tuple-element.135) | copy-start | bytes 4612
  566.4 8.7 %copy-start.11 = (bf16[392,768]{1,0:T(8,128)(2,1)S(1)}, bf16[392,768]{1,0:T(8,128)(2,1)}, u32[]{:S(2)}) copy-start(bf16[392,768]{1,0:T(8,128)(2,1)} %get-tuple-element.249) | copy-start | bytes 1806340
  567.4 8.5 %copy-start.10 = (f32[392,768]{1,0:T(8,128)S(1)}, f32[392,768]{1,0:T(8,128)}, u32[]{:S(2)}) copy-start(f32[392,768]{1,0:T(8,128)} %get-tuple-element.250) | copy-start | bytes 3612676
  (19 other events, 45.8 us)
